TPU v7x, 32 devices: a whole 2x2x4 slice. The times are simulated.
32 devices in a mesh: groups: 2 (over x), tensor: 16 (over z, y, core).
Axes of the slice: x: 2, y: 2, z: 4, core: 2. Of those that a mesh axis runs over, the one named last changes fastest.
Arguments:
- tokens: bfloat16 [768, 8192], P(('groups', 'tensor')), parts along dimension 0, may hold values from -6 to 6
- gate_weight: bfloat16 [8192, 14336], P(None, 'tensor'), may hold values from -0.0625 to 0.0625
- up_weight: bfloat16 [8192, 14336], P(None, 'tensor'), may hold values from -0.0625 to 0.0625
- down_weight: bfloat16 [14336, 8192], P('tensor'), may hold values from -0.046875 to 0.046875
- adapter_shrink: bfloat16 [16, 64, 8192], P('tensor'), may hold values from -0.0625 to 0.0625
- adapter_expand: bfloat16 [16, 64, 14336], P(None, None, 'tensor'), may hold values from -0.75 to 0.75
- adapter_list: int32 [28], P('groups'), parts along dimension 0, may hold values from 0 to 15, as said below
- block_slot: int32 [48], P('groups'), parts along dimension 0, may hold values from 0 to 13, never falling along the last dimension, each value on 1 to 6 neighbouring positions
- pool_slot: int32 [16], replicated, may hold values from 0 to 15, each once
Outputs:
- mixed: bfloat16 [768, 8192], P(('groups', 'tensor')), parts along dimension 0
There are 2 independent parts, one for each index of `groups`. A program takes and returns all parts, laid end to end along the dimension named above; an argument that names none is the same for every part. Nothing has to cross between parts.
Inputs may be any that keep to these rules, and one draw needn't show every extreme that they name: `adapter_list`: 14 distinct adapter ids. `block_slot`: never falls from block to block; every entry of the list has 1 to 6 blocks, one exactly 6. `pool_slot`: a permutation; pool row p lies on the device of tensor index p.
All inputs are finite; a program needn't handle non-finite values.
Results may differ from a plain program's by a relative error of at most 0.014.
Values may be sent and summed in bfloat16 or wider, within the bound.
A program may use at most 128 MiB of HBM per device.

v0:
```python
import jax
import jax.numpy as jnp
from jax import lax
from jax.sharding import PartitionSpec as P


def local(
    tokens,
    gate_weight,
    up_weight,
    down_weight,
    adapter_shrink,
    adapter_expand,
    adapter_list,
    block_slot,
    pool_slot,
):
    whole = lax.all_gather(tokens, "tensor", axis=0, tiled=True)
    token_count = whole.shape[0]
    count_of_blocks = block_slot.shape[0]
    block_rows = token_count // count_of_blocks
    rank_width = adapter_shrink.shape[1]
    per_device = adapter_shrink.shape[0]
    block_adapter = adapter_list[block_slot]
    self_index = lax.axis_index("tensor")
    resident_shrink = jnp.einsum(
        "td,prd->tpr", whole, adapter_shrink, preferred_element_type=jnp.float32
    )
    pool_rows = jnp.repeat(pool_slot[block_adapter], block_rows, total_repeat_length=token_count)
    slot_match = (pool_rows % per_device)[:, None] == jnp.arange(per_device, dtype=jnp.int32)[
        None, :
    ]
    owner_match = (pool_rows // per_device == self_index)[:, None]
    selector = jnp.logical_and(slot_match, owner_match).astype(jnp.float32)
    own_rows = jnp.einsum("tpr,tp->tr", resident_shrink, selector)
    reduced_rank_output = lax.psum(own_rows.astype(jnp.bfloat16), "tensor").astype(jnp.float32)
    reduced_rank_output = reduced_rank_output.astype(jnp.bfloat16)
    block_expand = adapter_expand[block_adapter]
    adapted = jnp.einsum(
        "bkr,brf->bkf",
        reduced_rank_output.reshape(count_of_blocks, block_rows, rank_width),
        block_expand,
        preferred_element_type=jnp.float32,
    )
    adapted = adapted.reshape(token_count, block_expand.shape[2])
    gate = jnp.dot(whole, gate_weight, preferred_element_type=jnp.float32)
    up = jnp.dot(whole, up_weight, preferred_element_type=jnp.float32) + adapted
    hidden = (jax.nn.silu(gate) * up).astype(jnp.bfloat16)
    return lax.psum_scatter(
        jnp.dot(hidden, down_weight, preferred_element_type=jnp.float32).astype(jnp.bfloat16),
        "tensor",
        scatter_dimension=0,
        tiled=True,
    )


def solution(mesh):
    return jax.shard_map(
        local,
        mesh=mesh,
        in_specs=(
            P(("groups", "tensor"), None),
            P(None, "tensor"),
            P(None, "tensor"),
            P("tensor", None),
            P("tensor", None, None),
            P(None, None, "tensor"),
            P("groups"),
            P("groups"),
            P(),
        ),
        out_specs=P(("groups", "tensor"), None),
        check_vma=False,
    )
```

profile of v0, /device:TPU:0, one launch (start us, length us, event | category | flops | bytes accessed | tf_op | source)
XLA Modules:
  0.0 268.3 jit_solution(15424071213157716922)
XLA Ops:
  6.5 0.7 all-gather.2.cloned.1.call-update
  7.3 0.0 reduce-scatter.2.cloned.1.call-start
  7.3 0.8 compare_select_fusion.9
  8.1 1.4 gather_fusion
  9.5 1.4 gather_fusion.1
  10.8 2.6 gather_fusion.2
  13.5 0.7 fusion.13
  14.1 0.7 fusion.12
  14.9 0.1 fusion.4
  14.9 4.6 %fusion.10 = (s32[384]{0:T(512)S(1)}, s32[384,1]{0,1:T(1,128)S(1)}) fusion(s32[]{:T(128)} %bitcast.22, s32[]{:T(128)} %bitcast.23, s32[]{:T(128)} %bitcast.24, s32[]{:T(128)} %bitcast.25, s32[]{:T(128)} %bitcast.26, s32[]{:T(128)} %bitcast.28, s32[]{:T(128)} %bitcast.27, s32[1,1,3,128]{3,2,1,0:T(4,128)S(1)} %get-tuple-element.37, ...), kind=kLoop, calls=%fused_computation.48 | loop fusion | flops 5376 | bytes 6172 | tf_op jit(solution)/shard_map/jit(_take)/gather | solution.py:29
  19.5 0.1 compare_reduce_fusion.16
  19.6 10.5 %fusion.9 = f32[384]{0:T(512)S(1)} fusion(pred[384]{0:T(512)(128)(4,1)S(1)} %get-tuple-element.33, pred[384]{0:T(512)(128)(4,1)S(1)} %get-tuple-element.32, pred[384]{0:T(512)(128)(4,1)S(1)} %get-tuple-element.31, pred[384]{0:T(512)(128)(4,1)S(1)} %get-tuple-element.30, pred[384]{0:T(512)(128)(4,1)S(1)} %get-tuple-element.29, ...), kind=kLoop, calls=%fused_computation.47 | loop fusion | flops 10752 | bytes 11220 | tf_op jit(solution)/shard_map/convert
  30.1 44.1 %all-gather.2.cloned.1.call-done = bf16[384,8192]{1,0:T(8,128)(2,1)} async-done(((bf16[24,8192]{1,0:T(8,128)(2,1)}), bf16[384,8192]{1,0:T(8,128)(2,1)}) %all-gather.2.cloned.1.call-update) | async-done | bytes 6291472 | tf_op jit(solution)/shard_map/all_gather | solution.py:18
  74.2 4.8 %fusion.2 = bf16[384,64]{0,1:T(8,128)(2,1)S(1)} fusion(bf16[384,8192]{1,0:T(8,128)(2,1)} %all-gather.2.cloned.1.call-done, bf16[1,64,8192]{2,1,0:T(8,128)(2,1)S(1)} %copy-done.1, f32[384]{0:T(512)S(1)} %fusion.9), kind=kOutput, calls=%fused_computation.8 | convolution fusion | flops 402702336 | bytes 7390720 | tf_op jit(solution)/shard_map/td,prd->tpr/dot_general | solution.py:26
  79.1 0.1 copy.11
  79.2 60.4 %psum.7 = bf16[24,16,64]{2,1,0:T(8,128)(2,1)S(1)} all-reduce(bf16[24,16,64]{2,1,0:T(8,128)(2,1)S(1)} %bitcast.75), channel_id=1, replica_groups=mesh['groups'=2,'tensor'=16] {'tensor'}, use_global_device_ids=true, to_apply=%region_0.1 | all-reduce | flops 24576 | bytes 98304 | tf_op jit(solution)/shard_map/psum | solution.py:36
  139.6 0.0 slice-start.2
  139.6 2.5 fusion.15
  142.1 0.0 slice-start.3
  142.1 16.0 %fusion.14 = f32[384,896]{1,0:T(8,128)S(1)} fusion(bf16[384,8192]{1,0:T(8,128)(2,1)} %all-gather.2.cloned.1.call-done, bf16[8192,896]{1,0:T(8,128)(2,1)} %param.12), kind=kOutput, calls=%fused_computation.53 | convolution fusion | flops 5637144576 | bytes 22347776 | tf_op jit(solution)/shard_map/dot_general | solution.py:46
  158.2 6.8 %fusion.1 = bf16[384,896]{1,0:T(8,128)(2,1)S(1)} fusion(f32[384,896]{1,0:T(8,128)S(1)} %bitcast.74, bf16[384,8192]{1,0:T(8,128)(2,1)S(1)} %bitcast.73, bf16[8192,896]{1,0:T(8,128)(2,1)S(1)} %bitcast.77, f32[384,896]{1,0:T(8,128)S(1)} %fusion.14), kind=kOutput, calls=%fused_computation.6 | convolution fusion | flops 5639553024 | bytes 24412160 | tf_op jit(solution)/shard_map/dot_general | solution.py:47
  165.0 14.0 %convolution_convert_fusion = bf16[384,8192]{1,0:T(8,128)(2,1)} fusion(bf16[384,896]{1,0:T(8,128)(2,1)S(1)} %fusion.1, bf16[896,8192]{1,0:T(8,128)(2,1)} %param.14), kind=kOutput, calls=%fused_computation.3 | convolution fusion | flops 5640290304 | bytes 21659648 | tf_op jit(solution)/shard_map/dot_general | solution.py:50
  179.0 0.0 reduce-scatter.2.cloned.1.call-update
  179.0 82.5 %reduce-scatter.2.cloned.1.call-done = bf16[24,8192]{1,0:T(8,128)(2,1)} async-done(((bf16[384,8192]{1,0:T(8,128)(2,1)}), bf16[24,8192]{1,0:T(8,128)(2,1)}) %reduce-scatter.2.cloned.1.call-update) | async-done | bytes 393232 | tf_op jit(solution)/shard_map/reduce_scatter | solution.py:49
  (23 shorter events, 0.1 us)
Async XLA Ops:
  6.5 4.3 %copy-start = (bf16[16,64,896]{2,1,0:T(8,128)(2,1)S(1)}, bf16[16,64,896]{2,1,0:T(8,128)(2,1)}, u32[]{:S(2)}) copy-start(bf16[16,64,896]{2,1,0:T(8,128)(2,1)} %param.16) | copy-start | bytes 5505028
  6.5 8.3 %copy-start.2 = (s32[3,128]{1,0:T(4,128)S(1)}, s32[3,128]{1,0:T(4,128)}, u32[]{:S(2)}) copy-start(s32[3,128]{1,0:T(4,128)} %constant.113.clone.1) | copy-start | bytes 4612
  6.5 67.7 %copy-start.1 = (bf16[1,64,8192]{2,1,0:T(8,128)(2,1)S(1)}, bf16[1,64,8192]{2,1,0:T(8,128)(2,1)}, u32[]{:S(2)}) copy-start(bf16[1,64,8192]{2,1,0:T(8,128)(2,1)} %param.15) | copy-start | bytes 3145732
  6.5 67.7 %all-gather.2.cloned.1.call-start = ((), (), s32[]{:S(2)}) async-start(), calls=%async_computation.1 | async-start | bytes 6684672 | tf_op jit(solution)/shard_map/all_gather | solution.py:18
  7.3 254.2 %reduce-scatter.2.cloned.1.call-start = ((), (), s32[]{:S(2)}) async-start(), calls=%async_computation.2 | async-start | bytes 6684672 | tf_op jit(solution)/shard_map/reduce_scatter | solution.py:49
  139.6 18.5 %slice-start = ((s8[6291456]{0:T(1024)(128)(4,1)}), s8[4194304]{0:T(1024)(128)(4,1)S(1)}, s32[]{:S(2)}) async-start(s8[6291456]{0:T(1024)(128)(4,1)} %bitcast.72), calls=%async_computation.3 | async-start | bytes 8388608
  139.6 18.5 %slice-start.2 = ((s8[14680064]{0:T(1024)(128)(4,1)}), s8[4194304]{0:T(1024)(128)(4,1)S(1)}, s32[]{:S(2)}) async-start(s8[14680064]{0:T(1024)(128)(4,1)} %bitcast.76), calls=%async_computation.5 | async-start | bytes 8388608
  142.1 16.0 %slice-start.1 = ((s8[6291456]{0:T(1024)(128)(4,1)}), s8[2097152]{0:T(1024)(128)(4,1)S(1)}, s32[]{:S(2)}) async-start(s8[6291456]{0:T(1024)(128)(4,1)} %bitcast.72), calls=%async_computation.4 | async-start | bytes 4194304
  142.1 16.0 %slice-start.3 = ((s8[14680064]{0:T(1024)(128)(4,1)}), s8[4194304]{0:T(1024)(128)(4,1)S(1)}, s32[]{:S(2)}) async-start(s8[14680064]{0:T(1024)(128)(4,1)} %bitcast.76), calls=%async_computation.6 | async-start | bytes 8388608
  142.1 16.0 %slice-start.4 = ((s8[14680064]{0:T(1024)(128)(4,1)}), s8[4194304]{0:T(1024)(128)(4,1)S(1)}, s32[]{:S(2)}) async-start(s8[14680064]{0:T(1024)(128)(4,1)} %bitcast.76), calls=%async_computation.7 | async-start | bytes 8388608
  142.1 16.0 %slice-start.5 = ((s8[14680064]{0:T(1024)(128)(4,1)}), s8[2097152]{0:T(1024)(128)(4,1)S(1)}, s32[]{:S(2)}) async-start(s8[14680064]{0:T(1024)(128)(4,1)} %bitcast.76), calls=%async_computation.8 | async-start | bytes 4194304
Sparse Core Ops, SparseCore 0:
  9.6 64.5 all-gather.1
  179.1 82.3 reduce-scatter.1
where the time goes:
time: 269 us; the launch traced here: 268 us
  waiting for transfers between devices  127 us (47%)
  blocking collectives  60.4 us (22%)
  matrix products  44.1 us (16%)
  other arithmetic  16 us (6%)
  between operations  13.6 us (5%)
  local copies, waits for them, and re-layouts  6.9 us (3%)
    reduce_scatter x1, waiting for transfers between devices, local(): lax.psum_scatter(jnp.dot(hidden, down_weight, preferred_element_type=jnp....  82.5 us
    psum x1, blocking collectives, local(): lax.psum(own_rows.astype(jnp.bfloat16), 'tensor').astype(jnp.float32)  60.4 us
    all_gather x1, waiting for transfers between devices, local(): whole = lax.all_gather(tokens, 'tensor', axis=0, tiled=True)  44.1 us
    dot_general x1, matrix products, local(): gate = jnp.dot(whole, gate_weight, preferred_element_type=jnp.float32)  16 us
    dot_general x1, matrix products, local(): jnp.dot(hidden, down_weight, preferred_element_type=jnp.float32)  14 us
    another operation x2, other arithmetic  10.5 us
    dot_general x1, matrix products, local(): up = jnp.dot(whole, up_weight, preferred_element_type=jnp.float32) + adapted  6.81 us
  transfers between devices with their start and end apart: 2, of which 2 were waited for; matrix products, arithmetic and copies ran while one was open for 8% of the time, Pallas kernels for 0%

commit v1 on v0

v1 whole, which is shorter than its diff:
```python
import functools
import jax
import jax.numpy as jnp
from jax import lax
from jax.experimental import pallas as pl
from jax.experimental.pallas import tpu as pltpu
from jax.sharding import PartitionSpec as P

MESH = pl.DeviceIdType.MESH
PH = 4
SUB = 2
F32 = jnp.float32
BF16 = jnp.bfloat16


def dot(a, b):
    return jnp.dot(a, b, preferred_element_type=F32)


def spans(width, unit):
    return [(lo, min(unit, width - lo)) for lo in range(0, width, unit)]


def kernel(
    fold,
    x_in,
    wg_hbm,
    wu_hbm,
    wd_hbm,
    shrink_hbm,
    expand_hbm,
    own_mask_hbm,
    row_pair_hbm,
    out,
    x,
    wg,
    wu,
    wd,
    s2,
    ex,
    own_mask,
    row_pair,
    accg,
    accu,
    accs,
    hid,
    sib,
    ring,
    ar_out,
    ar_in,
    load_sem,
    w_sem,
    s_sem,
    d_sem,
    m_sem,
    ag_send,
    ag_recv,
    fw_send,
    fw_recv,
    ar_send,
    ar_recv,
    sx_send,
    sx_recv,
    rs_send,
    rs_recv,
):
    rows = x_in.shape[0]
    n = x.shape[2] // rows
    width = x.shape[3]
    part = width // SUB
    half = PH * width
    ffw = wg.shape[3]
    stages = ar_out.shape[0]
    group = lax.axis_index("groups")
    me = lax.axis_index("tensor")
    core = me % 2
    chip = me // 2
    way = 1 - 2 * core
    if fold:
        zz, yy = chip // 2, chip % 2
        pos = yy * (n - 1 - zz) + (1 - yy) * zz
    else:
        pos = chip

    def chip_at(p):
        p = (p + 2 * n) % n
        if fold:
            up = p // (n // 2)
            return up * (2 * (n - 1 - p) + 1) + (1 - up) * 2 * p
        return p

    nxt = chip_at(pos + way) * 2 + core
    prv = chip_at(pos - way) * 2 + core
    other = me + way
    partners = [me + (1 - 2 * ((me // (1 << b)) % 2)) * (1 << b) for b in range(stages)]

    def rows_of(step):
        return pl.ds(pl.multiple_of(chip_at(pos - way * step) * rows, 16), rows)

    def load(ph):
        return pltpu.make_async_copy(
            x_in.at[:, pl.ds(pl.multiple_of(ph * width, 128), width)],
            x.at[core, ph, rows_of(0), :],
            load_sem.at[ph],
        )

    def ag(ph, m, step):
        ref = x.at[core, ph, rows_of(step), pl.ds(m * part, part)]
        return pltpu.make_async_remote_copy(
            src_ref=ref, dst_ref=ref, send_sem=ag_send.at[ph, m, step], recv_sem=ag_recv.at[ph, m, step],
            device_id=(group, nxt), device_id_type=MESH,
        )

    def fw(ph, m, step):
        ref = x.at[core, ph, rows_of(step), pl.ds(m * part, part)]
        return pltpu.make_async_remote_copy(
            src_ref=ref, dst_ref=ref, send_sem=fw_send.at[ph, m, step], recv_sem=fw_recv.at[ph, m, step],
            device_id=(group, other), device_id_type=MESH,
        )

    def w_copies(ph):
        return [
            pltpu.make_async_copy(src.at[h, ph], dst.at[h, ph], w_sem.at[i, h, ph])
            for h in range(2)
            for i, (src, dst) in enumerate(((wg_hbm, wg), (wu_hbm, wu)))
        ]

    def s_copies(ph):
        rank = shrink_hbm.shape[0]
        return [
            pltpu.make_async_copy(
                shrink_hbm.at[:, pl.ds(pl.multiple_of(h * half + ph * width, 128), width)],
                s2.at[h, ph, pl.ds(i * rank, rank), :],
                s_sem.at[i, h, ph],
            )
            for h in range(2)
            for i in range(2)
        ]

    def d_copy(h, ph):
        return pltpu.make_async_copy(
            wd_hbm.at[:, pl.ds(pl.multiple_of(h * half + ph * width, 128), width)], wd.at[h, ph], d_sem.at[h, ph]
        )

    m_copies = [
        pltpu.make_async_copy(src, dst, m_sem.at[i])
        for i, (src, dst) in enumerate(((expand_hbm, ex), (own_mask_hbm, own_mask), (row_pair_hbm, row_pair)))
    ]

    for ph in range(PH):
        load(ph).start()
    barrier = pltpu.get_barrier_semaphore()
    greet = [nxt, prv] + partners
    for dev in greet:
        pl.semaphore_signal(barrier, inc=1, device_id=(group, dev), device_id_type=MESH)
    pl.semaphore_wait(barrier, len(greet))

    def begin(ph):
        load(ph).wait()
        for m in range(SUB):
            ag(ph, m, 0).start()
            fw(ph, m, 0).start()

    begin(0)
    for ph in range(PH):
        for cp in w_copies(ph) + s_copies(ph):
            cp.start()
    for cp in m_copies:
        cp.start()
    for ph in range(PH):
        for h in range(2):
            d_copy(h, ph).start()
    accg[...] = jnp.zeros_like(accg)
    accu[...] = jnp.zeros_like(accu)
    accs[...] = jnp.zeros_like(accs)

    def ready(ph):
        def one(step, _):
            for m in range(SUB):
                fw(ph, m, step).wait_recv()
            return 0

        lax.fori_loop(0, n, one, 0)
        for cp in w_copies(ph) + s_copies(ph):
            cp.wait()

    def shrink_unit(ph):
        for h in range(2):
            accs[...] += lax.dot_general(
                x[h, ph], s2[h, ph], (((1,), (1,)), ((), ())), preferred_element_type=F32
            )

    def unit(ph, acc, w, lo, size):
        acc[:, lo : lo + size] += dot(x[0, ph], w[0, ph, :, lo : lo + size]) + dot(
            x[1, ph], w[1, ph, :, lo : lo + size]
        )

    units = [(acc, w, lo, size) for lo, size in spans(ffw, 256) for acc, w in ((accg, wg), (accu, wu))]
    share = -(-len(units) // (n - 1))

    def phase(ph, _):
        for step in range(1, n):
            if step == n - 1:

                @pl.when(ph + 1 < PH)
                def _():
                    begin(ph + 1)

            for m in range(SUB):
                ag(ph, m, step - 1).wait_recv()
                if step < n - 1:
                    ag(ph, m, step).start()
                fw(ph, m, step).start()

            mine = units[(step - 1) * share : step * share]
            if mine or step == 1:

                @pl.when(ph > 0)
                def _(mine=mine, step=step):
                    if step == 1:
                        ready(ph - 1)
                        shrink_unit(ph - 1)
                    for u in mine:
                        unit(ph - 1, *u)

        return 0

    lax.fori_loop(0, PH, phase, 0)

    last = PH - 1
    ready(last)
    shrink_unit(last)
    for cp in m_copies:
        cp.wait()
    owned = accs[...] * own_mask[...].astype(F32)
    tall = owned.shape[0] // 2
    packed = (owned[:tall] + owned[tall:]).astype(BF16)
    share = -(-len(units) // stages)
    for b in range(stages):
        ar_out[b] = packed
        cp = pltpu.make_async_remote_copy(
            src_ref=ar_out.at[b], dst_ref=ar_in.at[b], send_sem=ar_send.at[b], recv_sem=ar_recv.at[b],
            device_id=(group, partners[b]), device_id_type=MESH,
        )
        cp.start()
        for u in units[b * share : (b + 1) * share]:
            unit(last, *u)
        cp.wait()
        packed = (ar_out[b].astype(F32) + ar_in[b].astype(F32)).astype(BF16)

    rank = packed.shape[1] // 2
    whole = packed.astype(F32)
    turned = pltpu.roll(whole, rank, 1)
    low = lax.broadcasted_iota(jnp.int32, whole.shape, 1) < rank
    twice = jnp.concatenate([jnp.where(low, whole, turned), jnp.where(low, turned, whole)], axis=0).astype(BF16)

    def drain(ph, _):
        def one(step, _):
            for m in range(SUB):
                fw(ph, m, step).wait_send()
            return 0

        lax.fori_loop(0, n, one, 0)

        def two(step, _):
            for m in range(SUB):
                ag(ph, m, step).wait_send()
            return 0

        lax.fori_loop(0, n - 1, two, 0)
        return 0

    lax.fori_loop(0, PH, drain, 0)

    twice32 = twice.astype(F32)
    pair_of = row_pair[...].astype(F32)
    taken = ex.shape[0] // width
    for k in range(ex.shape[0] // (2 * rank)):
        lo = k * 2 * rank
        x[0, lo // width, :, lo % width : lo % width + 2 * rank] = jnp.where(pair_of == 2.0 * k, twice32, 0.0).astype(BF16)
    for lo, size in spans(ffw, 256):
        gate = accg[:, lo : lo + size]
        up = accu[:, lo : lo + size]
        for k in range(taken):
            up += dot(x[0, k], ex[k * width : (k + 1) * width, lo : lo + size])
        hid[:, lo : lo + size] = (gate / (1.0 + jnp.exp(-gate)) * up).astype(BF16)

    def sx(c):
        return pltpu.make_async_remote_copy(
            src_ref=x.at[1 - core, c], dst_ref=sib.at[c], send_sem=sx_send.at[c], recv_sem=sx_recv.at[c],
            device_id=(group, other), device_id_type=MESH,
        )

    def rs(c, step):
        return pltpu.make_async_remote_copy(
            src_ref=x.at[core, c, rows_of(step + 1), :], dst_ref=ring.at[c, step],
            send_sem=rs_send.at[c, step], recv_sem=rs_recv.at[c, step],
            device_id=(group, nxt), device_id_type=MESH,
        )

    def down(c):
        def fill(h):
            d_copy(h, c).wait()
            for lo, size in spans(width, 256):
                x[h, c, :, lo : lo + size] = dot(hid[...], wd[h, c, :, lo : lo + size]).astype(BF16)

        fill(1 - core)
        sx(c).start()
        fill(core)

    def slot(t, _):
        @pl.when(t < PH)
        def _():
            down(t)

        for c in range(PH):
            step = t - c

            @pl.when(step == 0)
            def _(c=c):
                sx(c).wait_recv()
                r = rows_of(1)
                x[core, c, r, :] = (x[core, c, r, :].astype(F32) + sib[c, r, :].astype(F32)).astype(BF16)
                rs(c, 0).start()

            @pl.when(jnp.logical_and(step > 0, step < n))
            def _(c=c, step=step):
                rs(c, step - 1).wait_recv()
                r = rows_of(step + 1)
                total = (
                    x[core, c, r, :].astype(F32) + sib[c, r, :].astype(F32) + ring[c, step - 1].astype(F32)
                ).astype(BF16)

                @pl.when(step < n - 1)
                def _():
                    x[core, c, r, :] = total
                    rs(c, step).start()

                @pl.when(step == n - 1)
                def _():
                    out[:, c * width : (c + 1) * width] = total

        return 0

    lax.fori_loop(0, n + PH - 1, slot, 0)
    for c in range(PH):
        sx(c).wait_send()

        def three(step, _, c=c):
            rs(c, step).wait_send()
            return 0

        lax.fori_loop(0, n - 1, three, 0)


def local(count, tokens, gate_weight, up_weight, down_weight, adapter_shrink, adapter_expand, adapter_list, block_slot, pool_slot):
    own_rows, model = tokens.shape
    half = model // 2
    width = half // PH
    n = count // 2
    rows = 2 * own_rows
    token_count = n * rows
    rank = adapter_shrink.shape[1]
    ffw = gate_weight.shape[1]
    adapters = adapter_expand.shape[0]
    stages = count.bit_length() - 1
    me = lax.axis_index("tensor")
    core = me % 2
    swap = [(i, i ^ 1) for i in range(count)]

    kept = lax.dynamic_slice_in_dim(tokens, core * half, half, 1)
    given = lax.dynamic_slice_in_dim(tokens, (1 - core) * half, half, 1)
    got = lax.ppermute(given, "tensor", swap)
    x_in = jnp.where(core == 0, jnp.concatenate([kept, got]), jnp.concatenate([got, kept]))

    block_adapter = adapter_list[block_slot]
    block_rows = token_count // block_slot.shape[0]
    row_adapter = jnp.repeat(block_adapter, block_rows, total_repeat_length=token_count)
    row_pool = jnp.repeat(pool_slot[block_adapter], block_rows, total_repeat_length=token_count)
    second = jnp.arange(token_count) >= token_count // 2
    lane = jnp.arange(2 * rank) >= rank
    own_mask = jnp.logical_and((row_pool == me)[:, None], second[:, None] == lane[None, :]).astype(BF16)
    row_pair = (row_adapter[:, None] - lane[None, :].astype(jnp.int32)).astype(BF16)

    dma = pltpu.SemaphoreType.DMA
    flops = 2 * token_count * model * ffw * 3
    reduced = pl.pallas_call(
        functools.partial(kernel, count == 16),
        out_shape=jax.ShapeDtypeStruct((rows, half), BF16),
        in_specs=[pl.BlockSpec(memory_space=pl.ANY)] * 8,
        out_specs=pl.BlockSpec(memory_space=pltpu.VMEM),
        scratch_shapes=[
            pltpu.VMEM((2, PH, token_count, width), BF16),
            pltpu.VMEM((2, PH, width, ffw), BF16),
            pltpu.VMEM((2, PH, width, ffw), BF16),
            pltpu.VMEM((2, PH, ffw, width), BF16),
            pltpu.VMEM((2, PH, 2 * rank, width), BF16),
            pltpu.VMEM((adapters * rank, ffw), BF16),
            pltpu.VMEM((token_count, 2 * rank), BF16),
            pltpu.VMEM((token_count, 2 * rank), BF16),
            pltpu.VMEM((token_count, ffw), F32),
            pltpu.VMEM((token_count, ffw), F32),
            pltpu.VMEM((token_count, 2 * rank), F32),
            pltpu.VMEM((token_count, ffw), BF16),
            pltpu.VMEM((PH, token_count, width), BF16),
            pltpu.VMEM((PH, n - 1, rows, width), BF16),
            pltpu.VMEM((stages, token_count // 2, 2 * rank), BF16),
            pltpu.VMEM((stages, token_count // 2, 2 * rank), BF16),
            dma((PH,)),
            dma((2, 2, PH)),
            dma((2, 2, PH)),
            dma((2, PH)),
            dma((3,)),
            dma((PH, SUB, n - 1)),
            dma((PH, SUB, n - 1)),
            dma((PH, SUB, n)),
            dma((PH, SUB, n)),
            dma((stages,)),
            dma((stages,)),
            dma((PH,)),
            dma((PH,)),
            dma((PH, n - 1)),
            dma((PH, n - 1)),
        ],
        compiler_params=pltpu.CompilerParams(
            collective_id=0, has_side_effects=True, vmem_limit_bytes=63 * 1024 * 1024
        ),
        cost_estimate=pl.CostEstimate(flops=flops, bytes_accessed=6 * model * ffw, transcendentals=token_count * ffw),
    )(
        x_in,
        gate_weight.reshape(2, PH, width, ffw),
        up_weight.reshape(2, PH, width, ffw),
        down_weight,
        adapter_shrink[0],
        adapter_expand.reshape(adapters * rank, ffw),
        own_mask,
        row_pair,
    )
    mine = lax.dynamic_slice_in_dim(reduced, core * own_rows, own_rows, 0)
    theirs = lax.dynamic_slice_in_dim(reduced, (1 - core) * own_rows, own_rows, 0)
    got = lax.ppermute(theirs, "tensor", swap)
    return jnp.where(core == 0, jnp.concatenate([mine, got], 1), jnp.concatenate([got, mine], 1))


def solution(mesh):
    return jax.shard_map(
        functools.partial(local, mesh.shape["tensor"]),
        mesh=mesh,
        in_specs=(
            P(("groups", "tensor"), None),
            P(None, "tensor"),
            P(None, "tensor"),
            P("tensor", None),
            P("tensor", None, None),
            P(None, None, "tensor"),
            P("groups"),
            P("groups"),
            P(),
        ),
        out_specs=P(("groups", "tensor"), None),
        check_vma=False,
    )
```

time: 269 us -> 191 us (0.71)
  Pallas kernels: 0 us -> 147 us
  waiting for transfers between devices: 127 us -> 1.43 us
  blocking collectives: 60.4 us -> 0 us
  matrix products: 44.1 us -> 0 us
  other arithmetic: 16 us -> 34.6 us
  between operations: 13.6 us -> 0.06 us
    pallas_call x0 -> x1, Pallas kernels: none -> 147 us  [local(): pl.pallas_call(functools.partial(kernel, count == 16), out_shape=jax.Shap...]
    reduce_scatter x1 -> x0, waiting for transfers between devices: 82.5 us -> none  [local(): lax.psum_scatter(jnp.dot(hidden, down_weight, preferred_element_type=jnp....]
    psum x1 -> x0, blocking collectives: 60.4 us -> none  [local(): lax.psum(own_rows.astype(jnp.bfloat16), 'tensor').astype(jnp.float32)]
    all_gather x1 -> x0, waiting for transfers between devices: 44.1 us -> none  [local(): whole = lax.all_gather(tokens, 'tensor', axis=0, tiled=True)]
    dot_general x5 -> x0, matrix products: 44.1 us -> none  [the longest x1 16 us: local(): gate = jnp.dot(whole, gate_weight, preferred_element_type=jnp.float32)]
    select_n x0 -> x3, other arithmetic: none -> 17.2 us  [the longest x1 15.6 us: local(): jnp.repeat(block_adapter, block_rows, total_repeat_length=token_count)]
    eq x0 -> x1, other arithmetic: none -> 15.1 us  [local(): row_pool == me]
    another operation x2 -> x1, other arithmetic: 10.5 us -> 0.01 us
  transfers between devices with their start and end apart: 2 -> 2, of which waited for: 2 -> 1; matrix products, arithmetic and copies ran while one was open for 8% -> 20% of each run, Pallas kernels for 0% -> 0%
where the time goes in v1:
time: 191 us
  Pallas kernels  147 us (77%)
  other arithmetic  34.6 us (18%)
  local copies, waits for them, and re-layouts  6.95 us (4%)
    pallas_call x1, Pallas kernels, local(): pl.pallas_call(functools.partial(kernel, count == 16), out_shape=jax.Shap...  147 us
    select_n x1, other arithmetic, local(): jnp.repeat(block_adapter, block_rows, total_repeat_length=token_count)  15.6 us
    eq x1, other arithmetic, local(): row_pool == me  15.1 us
  transfers between devices with their start and end apart: 2, of which 1 were waited for; matrix products, arithmetic and copies ran while one was open for 20% of the time, Pallas kernels for 0%

profile of v1, /device:TPU:0, one launch (start us, length us, event | category | flops | bytes accessed | tf_op | source)
XLA Modules:
  0.0 190.5 jit_solution(229596679872089215)
XLA Ops:
  0.0 0.0 copy-start
  0.0 1.1 constant_dynamic-slice_fusion.3
  1.1 0.5 collective-permute-start
  1.6 0.7 compare_select_fusion.2
  2.3 0.0 copy-done
  2.3 0.7 gather_fusion
  3.0 0.7 fusion.5
  3.7 1.4 gather_fusion.1
  5.0 0.7 fusion.3
  5.7 0.7 fusion.2
  6.4 0.7 fusion.4
  7.1 15.6 %select_select_fusion = (s32[384]{0:T(512)S(1)}, pred[384]{0:T(512)(128)(4,1)S(1)}, pred[384]{0:T(512)(128)(4,1)S(1)}, pred[384]{0:T(512)(128)(4,1)S(1)}, pred[3...) fusion(s32[]{:T(128)} %bitcast.54, s32[]{:T(128)} %bitcast.53, ...), kind=kLoop, calls=%fused_computation.11 | loop fusion | flops 21120 | bytes 12396 | tf_op jit(solution)/shard_map/jit(_take)/select_n | solution.py:378
  22.7 0.8 subtract_convert_fusion.row_pair_hbm
  23.5 15.1 %select_compare_fusion = pred[384]{0:T(512)(128)(4,1)S(1)} fusion(pred[384]{0:T(512)(128)(4,1)S(1)} %get-tuple-element.50, pred[384]{0:T(512)(128)(4,1)S(1)} %get-tuple-element.49, pred[384]{0:T(512)(128)(4,1)S(1)} %get-tuple-element.48, pred[384]{0:T(512)(128)(4,1)S(1)} %get-tuple-element.47, pred[384]{0:T(512)(128)(4,1)S(1)} %get-tuple-element.46, ...), kind=kLoop, calls=%fused_computation.12 | loop fusion | flops 9600 | bytes 9700 | tf_op jit(solution)/shard_map/eq | solution.py:382
  38.6 0.8 and_convert_fusion.own_mask_hbm
  39.4 0.0 collective-permute-done
  39.4 0.8 maximum_select_fusion.x_in
  40.2 146.9 %shard_map.91 = bf16[48,4096]{1,0:T(8,128)(2,1)} custom-call(bf16[48,4096]{1,0:T(8,128)(2,1)} %maximum_select_fusion.x_in, bf16[2,4,1024,896]{3,2,1,0:T(8,128)(2,1)} %bitcast.58, bf16[2,4,1024,896]{3,2,1,0:T(8,128)(2,1)} %bitcast.59, bf16[896,8192]{1,0:T(8,128)(2,1)} %wd_hbm.1, bf16[64,8192]{1,0:T(8,128)(2,1)} %bitcast.61, bf16[1024,896]{1,0:T(8,128)(2,1)} %bitcast.60, ...), custom_call_target="tpu_custom_call" | custom-call | flops 16911433728 | bytes 44040192 | tf_op jit(solution)/shard_map/pallas_call | solution.py:387
  187.1 1.1 constant_dynamic-slice_fusion.1
  188.2 0.1 collective-permute-start.1
  188.3 1.4 collective-permute-done.1
  189.7 0.8 maximum_select_fusion.1
  (7 shorter events, 0.0 us)
Async XLA Ops:
  0.0 2.3 %copy-start = (s32[14]{0:T(128)S(1)}, s32[14]{0:T(128)}, u32[]{:S(2)}) copy-start(s32[14]{0:T(128)} %param.21) | copy-start | bytes 172
  1.1 38.3 %collective-permute-start = (bf16[24,4096]{1,0:T(8,128)(2,1)S(1)}, bf16[24,4096]{1,0:T(8,128)(2,1)S(1)}, u32[]{:S(2)}, u32[]{:S(2)}) collective-permute-start(bf16[24,4096]{1,0:T(8,128)(2,1)S(1)} %get-tuple-element.54), channel_id=1, source_target_pairs={{0,1},{1,0},{2,3},{3,2},{4,5},{5,4},{6,7},{7,6},{8,9},{9,8},{10,11... | collective-permute-start | bytes 589832 | tf_op jit(solution)/shard_map/ppermute | solution.py:373
  188.2 1.5 collective-permute-start.1

commit v2 on v1

--- a/solution.py
+++ b/solution.py
@@ -8,7 +8,7 @@
 
 MESH = pl.DeviceIdType.MESH
 PH = 4
-SUB = 2
+SUB = 1
 F32 = jnp.float32
 BF16 = jnp.bfloat16
 
@@ -29,8 +29,9 @@
     wd_hbm,
     shrink_hbm,
     expand_hbm,
-    own_mask_hbm,
-    row_pair_hbm,
+    adapter_list,
+    block_slot,
+    pool_slot,
     out,
     x,
     wg,
@@ -142,10 +143,7 @@
             wd_hbm.at[:, pl.ds(pl.multiple_of(h * half + ph * width, 128), width)], wd.at[h, ph], d_sem.at[h, ph]
         )
 
-    m_copies = [
-        pltpu.make_async_copy(src, dst, m_sem.at[i])
-        for i, (src, dst) in enumerate(((expand_hbm, ex), (own_mask_hbm, own_mask), (row_pair_hbm, row_pair)))
-    ]
+    m_copies = [pltpu.make_async_copy(expand_hbm, ex, m_sem.at[0])]
 
     for ph in range(PH):
         load(ph).start()
@@ -161,7 +159,6 @@
             ag(ph, m, 0).start()
             fw(ph, m, 0).start()
 
-    begin(0)
     for ph in range(PH):
         for cp in w_copies(ph) + s_copies(ph):
             cp.start()
@@ -173,6 +170,20 @@
     accg[...] = jnp.zeros_like(accg)
     accu[...] = jnp.zeros_like(accu)
     accs[...] = jnp.zeros_like(accs)
+    blocks = block_slot.shape[0]
+    block_rows = own_mask.shape[0] // blocks
+    upper = (lax.broadcasted_iota(jnp.int32, (block_rows, own_mask.shape[1]), 1) >= own_mask.shape[1] // 2).astype(F32)
+
+    def marks(b, _):
+        adapter = adapter_list[block_slot[b]]
+        here = (pool_slot[adapter] == me).astype(F32)
+        second = (b >= blocks // 2).astype(F32)
+        at = pl.ds(pl.multiple_of(b * block_rows, 16), block_rows)
+        own_mask[at, :] = here * (1.0 - jnp.abs(upper - second))
+        row_pair[at, :] = adapter.astype(F32) - upper
+        return 0
+
+    lax.fori_loop(0, blocks, marks, 0)
 
     def ready(ph):
         def one(step, _):
@@ -196,43 +207,42 @@
         )
 
     units = [(acc, w, lo, size) for lo, size in spans(ffw, 256) for acc, w in ((accg, wg), (accu, wu))]
-    share = -(-len(units) // (n - 1))
-
-    def phase(ph, _):
-        for step in range(1, n):
-            if step == n - 1:
-
-                @pl.when(ph + 1 < PH)
-                def _():
-                    begin(ph + 1)
-
-            for m in range(SUB):
-                ag(ph, m, step - 1).wait_recv()
-                if step < n - 1:
-                    ag(ph, m, step).start()
-                fw(ph, m, step).start()
-
-            mine = units[(step - 1) * share : step * share]
-            if mine or step == 1:
-
-                @pl.when(ph > 0)
-                def _(mine=mine, step=step):
-                    if step == 1:
-                        ready(ph - 1)
-                        shrink_unit(ph - 1)
-                    for u in mine:
-                        unit(ph - 1, *u)
+    def wave(t, _):
+        for c in range(PH):
+            step = t - c
+
+            @pl.when(step == 0)
+            def _(c=c):
+                begin(c)
+
+            @pl.when(jnp.logical_and(step > 0, step < n))
+            def _(c=c, step=step):
+                for m in range(SUB):
+                    ag(c, m, step - 1).wait_recv()
+
+                    @pl.when(step < n - 1)
+                    def _(m=m):
+                        ag(c, m, step).start()
+
+                    fw(c, m, step).start()
+
+        @pl.when(t >= n)
+        def _():
+            ready(t - n)
+            shrink_unit(t - n)
+            for u in units:
+                unit(t - n, *u)
 
         return 0
 
-    lax.fori_loop(0, PH, phase, 0)
+    lax.fori_loop(0, n + PH - 1, wave, 0)
 
     last = PH - 1
     ready(last)
     shrink_unit(last)
     for cp in m_copies:
         cp.wait()
-    owned = accs[...] * own_mask[...].astype(F32)
+    owned = accs[...] * own_mask[...]
     tall = owned.shape[0] // 2
     packed = (owned[:tall] + owned[tall:]).astype(BF16)
     share = -(-len(units) // stages)
@@ -273,7 +283,7 @@
     lax.fori_loop(0, PH, drain, 0)
 
     twice32 = twice.astype(F32)
-    pair_of = row_pair[...].astype(F32)
+    pair_of = row_pair[...]
     taken = ex.shape[0] // width
     for k in range(ex.shape[0] // (2 * rank)):
         lo = k * 2 * rank
@@ -308,41 +318,38 @@
         sx(c).start()
         fill(core)
 
-    def slot(t, _):
-        @pl.when(t < PH)
+    def kick(c):
+        sx(c).wait_recv()
+        r = rows_of(1)
+        x[core, c, r, :] = (x[core, c, r, :].astype(F32) + sib[c, r, :].astype(F32)).astype(BF16)
+        rs(c, 0).start()
+
+    def lead(c, _):
+        down(c)
+
+        @pl.when(c > 0)
         def _():
-            down(t)
-
+            kick(c - 1)
+
+        return 0
+
+    lax.fori_loop(0, PH, lead, 0)
+    kick(PH - 1)
+
+    def total(c, step):
+        rs(c, step - 1).wait_recv()
+        r = rows_of(step + 1)
+        return (x[core, c, r, :].astype(F32) + sib[c, r, :].astype(F32) + ring[c, step - 1].astype(F32)).astype(BF16)
+
+    def hop(step, _):
         for c in range(PH):
-            step = t - c
-
-            @pl.when(step == 0)
-            def _(c=c):
-                sx(c).wait_recv()
-                r = rows_of(1)
-                x[core, c, r, :] = (x[core, c, r, :].astype(F32) + sib[c, r, :].astype(F32)).astype(BF16)
-                rs(c, 0).start()
-
-            @pl.when(jnp.logical_and(step > 0, step < n))
-            def _(c=c, step=step):
-                rs(c, step - 1).wait_recv()
-                r = rows_of(step + 1)
-                total = (
-                    x[core, c, r, :].astype(F32) + sib[c, r, :].astype(F32) + ring[c, step - 1].astype(F32)
-                ).astype(BF16)
-
-                @pl.when(step < n - 1)
-                def _():
-                    x[core, c, r, :] = total
-                    rs(c, step).start()
-
-                @pl.when(step == n - 1)
-                def _():
-                    out[:, c * width : (c + 1) * width] = total
-
+            x[core, c, rows_of(step + 1), :] = total(c, step)
+            rs(c, step).start()
         return 0
 
-    lax.fori_loop(0, n + PH - 1, slot, 0)
+    lax.fori_loop(1, n - 1, hop, 0)
+    for c in range(PH):
+        out[:, c * width : (c + 1) * width] = total(c, n - 1)
     for c in range(PH):
         sx(c).wait_send()
 
@@ -364,30 +371,20 @@
     ffw = gate_weight.shape[1]
     adapters = adapter_expand.shape[0]
     stages = count.bit_length() - 1
-    me = lax.axis_index("tensor")
-    core = me % 2
+    core = lax.axis_index("tensor") % 2
     swap = [(i, i ^ 1) for i in range(count)]
 
     kept = lax.dynamic_slice_in_dim(tokens, core * half, half, 1)
     given = lax.dynamic_slice_in_dim(tokens, (1 - core) * half, half, 1)
     got = lax.ppermute(given, "tensor", swap)
     x_in = jnp.where(core == 0, jnp.concatenate([kept, got]), jnp.concatenate([got, kept]))
-
-    block_adapter = adapter_list[block_slot]
-    block_rows = token_count // block_slot.shape[0]
-    row_adapter = jnp.repeat(block_adapter, block_rows, total_repeat_length=token_count)
-    row_pool = jnp.repeat(pool_slot[block_adapter], block_rows, total_repeat_length=token_count)
-    second = jnp.arange(token_count) >= token_count // 2
-    lane = jnp.arange(2 * rank) >= rank
-    own_mask = jnp.logical_and((row_pool == me)[:, None], second[:, None] == lane[None, :]).astype(BF16)
-    row_pair = (row_adapter[:, None] - lane[None, :].astype(jnp.int32)).astype(BF16)
 
     dma = pltpu.SemaphoreType.DMA
     flops = 2 * token_count * model * ffw * 3
     reduced = pl.pallas_call(
         functools.partial(kernel, count == 16),
         out_shape=jax.ShapeDtypeStruct((rows, half), BF16),
-        in_specs=[pl.BlockSpec(memory_space=pl.ANY)] * 8,
+        in_specs=[pl.BlockSpec(memory_space=pl.ANY)] * 6 + [pl.BlockSpec(memory_space=pltpu.SMEM)] * 3,
         out_specs=pl.BlockSpec(memory_space=pltpu.VMEM),
         scratch_shapes=[
             pltpu.VMEM((2, PH, token_count, width), BF16),
@@ -396,8 +393,8 @@
             pltpu.VMEM((2, PH, ffw, width), BF16),
             pltpu.VMEM((2, PH, 2 * rank, width), BF16),
             pltpu.VMEM((adapters * rank, ffw), BF16),
-            pltpu.VMEM((token_count, 2 * rank), BF16),
-            pltpu.VMEM((token_count, 2 * rank), BF16),
+            pltpu.VMEM((token_count, 2 * rank), F32),
+            pltpu.VMEM((token_count, 2 * rank), F32),
             pltpu.VMEM((token_count, ffw), F32),
             pltpu.VMEM((token_count, ffw), F32),
             pltpu.VMEM((token_count, 2 * rank), F32),
@@ -410,7 +407,7 @@
             dma((2, 2, PH)),
             dma((2, 2, PH)),
             dma((2, PH)),
-            dma((3,)),
+            dma((1,)),
             dma((PH, SUB, n - 1)),
             dma((PH, SUB, n - 1)),
             dma((PH, SUB, n)),
@@ -433,8 +430,9 @@
         down_weight,
         adapter_shrink[0],
         adapter_expand.reshape(adapters * rank, ffw),
-        own_mask,
-        row_pair,
+        adapter_list,
+        block_slot,
+        pool_slot,
     )
     mine = lax.dynamic_slice_in_dim(reduced, core * own_rows, own_rows, 0)
     theirs = lax.dynamic_slice_in_dim(reduced, (1 - core) * own_rows, own_rows, 0)

time: 191 us -> 114 us (0.60)
  Pallas kernels: 147 us -> 107 us
  other arithmetic: 34.6 us -> 1.65 us
  local copies, waits for them, and re-layouts: 6.95 us -> 2.1 us
    pallas_call x1, Pallas kernels: 147 us -> 107 us  [local(): pl.pallas_call(functools.partial(kernel, count == 16), out_shape=jax.Shap...]
    select_n x3 -> x0, other arithmetic: 16.3 us -> none  [the longest x1 15.6 us: local(): jnp.repeat(block_adapter, block_rows, total_repeat_length=token_count)]
    eq x1 -> x0, other arithmetic: 15.1 us -> none  [local(): row_pool == me]
    gather x6 -> x0, local copies, waits for them, and re-layouts: 4.83 us -> none  [the longest x2 1.4 us: local(): jnp.repeat(pool_slot[block_adapter], block_rows, total_repeat_length=toke...]
  transfers between devices with their start and end apart: 2 -> 2, of which waited for: 1 -> 2; matrix products, arithmetic and copies ran while one was open for 20% -> 0% of each run, Pallas kernels for 0% -> 0%
where the time goes in v2:
time: 114 us
  Pallas kernels  107 us (94%)
  waiting for transfers between devices  2.5 us (2%)
  local copies, waits for them, and re-layouts  2.1 us (2%)
  other arithmetic  1.65 us (1%)
    pallas_call x1, Pallas kernels, local(): pl.pallas_call(functools.partial(kernel, count == 16), out_shape=jax.Shap...  107 us
  transfers between devices with their start and end apart: 2, of which 2 were waited for; matrix products, arithmetic and copies ran while one was open for 0% of the time, Pallas kernels for 0%

profile of v2, /device:TPU:0, one launch (start us, length us, event | category | flops | bytes accessed | tf_op | source)
XLA Modules:
  0.0 114.0 jit_solution(13943545036672469266)
XLA Ops:
  0.0 1.0 constant_dynamic-slice_fusion.3
  1.1 0.5 collective-permute-start
  1.6 1.1 collective-permute-done
  2.6 0.8 maximum_select_fusion.x_in
  3.5 107.2 %shard_map.91 = bf16[48,4096]{1,0:T(8,128)(2,1)} custom-call(bf16[48,4096]{1,0:T(8,128)(2,1)} %maximum_select_fusion.x_in, bf16[2,4,1024,896]{3,2,1,0:T(8,128)(2,1)} %bitcast.4, bf16[2,4,1024,896]{3,2,1,0:T(8,128)(2,1)} %bitcast.5, bf16[896,8192]{1,0:T(8,128)(2,1)} %wd_hbm.1, bf16[64,8192]{1,0:T(8,128)(2,1)} %bitcast.7, bf16[1024,896]{1,0:T(8,128)(2,1)} %bitcast.6, ...), custom_call_target="tpu_custom_call" | custom-call | flops 16911433728 | bytes 44040192 | tf_op jit(solution)/shard_map/pallas_call | solution.py:384
  110.6 1.1 constant_dynamic-slice_fusion.1
  111.7 0.1 collective-permute-start.1
  111.8 1.4 %collective-permute-done.1 = bf16[24,4096]{1,0:T(8,128)(2,1)S(1)} collective-permute-done((bf16[24,4096]{1,0:T(8,128)(2,1)S(1)}, bf16[24,4096]{1,0:T(8,128)(2,1)S(1)}, u32[]{:S(2)}, u32[]{:S(2)}) %collective-permute-start.1) | collective-permute-done | bytes 196640 | tf_op jit(solution)/shard_map/ppermute | solution.py:439
  113.2 0.8 maximum_select_fusion.1
Async XLA Ops:
  1.1 1.6 %collective-permute-start = (bf16[24,4096]{1,0:T(8,128)(2,1)S(1)}, bf16[24,4096]{1,0:T(8,128)(2,1)S(1)}, u32[]{:S(2)}, u32[]{:S(2)}) collective-permute-start(bf16[24,4096]{1,0:T(8,128)(2,1)S(1)} %get-tuple-element.8), channel_id=1, source_target_pairs={{0,1},{1,0},{2,3},{3,2},{4,5},{5,4},{6,7},{7,6},{8,9},{9,8},{10,11... | collective-permute-start | bytes 589832 | tf_op jit(solution)/shard_map/ppermute | solution.py:379
  111.7 1.5 %collective-permute-start.1 = (bf16[24,4096]{1,0:T(8,128)(2,1)S(1)}, bf16[24,4096]{1,0:T(8,128)(2,1)S(1)}, u32[]{:S(2)}, u32[]{:S(2)}) collective-permute-start(bf16[24,4096]{1,0:T(8,128)(2,1)S(1)} %get-tuple-element.6), channel_id=1, source_target_pairs={{0,1},{1,0},{2,3},{3,2},{4,5},{5,4},{6,7},{7,6},{8,9},{9,8},{10,11... | collective-permute-start | bytes 589832 | tf_op jit(solution)/shard_map/ppermute | solution.py:439

commit v3 on v2

--- a/solution.py
+++ b/solution.py
@@ -8,7 +8,7 @@
 
 MESH = pl.DeviceIdType.MESH
 PH = 4
-SUB = 1
+SUB = 2
 F32 = jnp.float32
 BF16 = jnp.bfloat16
 

time: 114 us -> 113 us (level)
    pallas_call x1, Pallas kernels: 107 us -> 106 us  [local(): pl.pallas_call(functools.partial(kernel, count == 16), out_shape=jax.Shap...]
where the time goes in v3:
time: 113 us
  Pallas kernels  106 us (94%)
  waiting for transfers between devices  2.5 us (2%)
  local copies, waits for them, and re-layouts  2.1 us (2%)
  other arithmetic  1.65 us (1%)
    pallas_call x1, Pallas kernels, local(): pl.pallas_call(functools.partial(kernel, count == 16), out_shape=jax.Shap...  106 us
  transfers between devices with their start and end apart: 2, of which 2 were waited for; matrix products, arithmetic and copies ran while one was open for 0% of the time, Pallas kernels for 0%

profile of v3, /device:TPU:0, one launch (start us, length us, event | category | flops | bytes accessed | tf_op | source)
XLA Modules:
  0.0 112.7 jit_solution(6960649611894494501)
XLA Ops:
  0.0 1.0 constant_dynamic-slice_fusion.3
  1.1 0.5 collective-permute-start
  1.6 1.1 collective-permute-done
  2.6 0.8 maximum_select_fusion.x_in
  3.5 105.9 %shard_map.91 = bf16[48,4096]{1,0:T(8,128)(2,1)} custom-call(bf16[48,4096]{1,0:T(8,128)(2,1)} %maximum_select_fusion.x_in, bf16[2,4,1024,896]{3,2,1,0:T(8,128)(2,1)} %bitcast.4, bf16[2,4,1024,896]{3,2,1,0:T(8,128)(2,1)} %bitcast.5, bf16[896,8192]{1,0:T(8,128)(2,1)} %wd_hbm.1, bf16[64,8192]{1,0:T(8,128)(2,1)} %bitcast.7, bf16[1024,896]{1,0:T(8,128)(2,1)} %bitcast.6, ...), custom_call_target="tpu_custom_call" | custom-call | flops 16911433728 | bytes 44040192 | tf_op jit(solution)/shard_map/pallas_call | solution.py:384
  109.3 1.1 constant_dynamic-slice_fusion.1
  110.4 0.1 collective-permute-start.1
  110.5 1.4 %collective-permute-done.1 = bf16[24,4096]{1,0:T(8,128)(2,1)S(1)} collective-permute-done((bf16[24,4096]{1,0:T(8,128)(2,1)S(1)}, bf16[24,4096]{1,0:T(8,128)(2,1)S(1)}, u32[]{:S(2)}, u32[]{:S(2)}) %collective-permute-start.1) | collective-permute-done | bytes 196640 | tf_op jit(solution)/shard_map/ppermute | solution.py:439
  111.9 0.8 maximum_select_fusion.1
Async XLA Ops:
  1.1 1.6 %collective-permute-start = (bf16[24,4096]{1,0:T(8,128)(2,1)S(1)}, bf16[24,4096]{1,0:T(8,128)(2,1)S(1)}, u32[]{:S(2)}, u32[]{:S(2)}) collective-permute-start(bf16[24,4096]{1,0:T(8,128)(2,1)S(1)} %get-tuple-element.8), channel_id=1, source_target_pairs={{0,1},{1,0},{2,3},{3,2},{4,5},{5,4},{6,7},{7,6},{8,9},{9,8},{10,11... | collective-permute-start | bytes 589832 | tf_op jit(solution)/shard_map/ppermute | solution.py:379
  110.4 1.5 %collective-permute-start.1 = (bf16[24,4096]{1,0:T(8,128)(2,1)S(1)}, bf16[24,4096]{1,0:T(8,128)(2,1)S(1)}, u32[]{:S(2)}, u32[]{:S(2)}) collective-permute-start(bf16[24,4096]{1,0:T(8,128)(2,1)S(1)} %get-tuple-element.6), channel_id=1, source_target_pairs={{0,1},{1,0},{2,3},{3,2},{4,5},{5,4},{6,7},{7,6},{8,9},{9,8},{10,11... | collective-permute-start | bytes 589832 | tf_op jit(solution)/shard_map/ppermute | solution.py:439
